TPU v7x, 512 devices: a whole 4x8x8 slice. The times are simulated.
512 devices in a mesh: row: 16 (over z, core), col: 32 (over y, x).
Axes of the slice: x: 4, y: 8, z: 8, core: 2. Of those that a mesh axis runs over, the one named last changes fastest.
Arguments:
- features: bfloat16 [65536, 256], P('col', 'row'), may hold values from -6 to 6
- weight: bfloat16 [256, 256], replicated, may hold values from -0.375 to 0.375
- cotangent: bfloat16 [65536, 256], P(('row', 'col')), may hold values from -6 to 6
- tile_values: bfloat16 [16, 32, 96, 128, 128], P('row', 'col'), may hold values from -0.0546875 to 0.0546875
- tile_coords: int32 [16, 32, 96, 2], P('row', 'col'), may hold values from 0 to 31, as said below
- tile_count: int32 [16, 32], P('row', 'col'), may hold values from 24 to 96
Outputs:
- activations: bfloat16 [65536, 256], P(('row', 'col'))
- grad_features: bfloat16 [65536, 256], P('col', 'row')
- grad_weight: float32 [256, 256], replicated
Inputs may be any that keep to these rules, and one draw needn't show every extreme that they name: `tile_coords`: within a block the slots name distinct tiles; tile rows are below 32 and tile columns below 16.
All inputs are finite; a program needn't handle non-finite values.
Results may differ from a plain program's by a relative error of at most 0.03.
Values may be sent and summed in bfloat16 or wider, within the bound.
No kernel may reach another device: no remote copies, remote signals or barrier semaphores. Data moves between devices by JAX's collectives and lax.ppermute only.
A program may use at most 64 MiB of HBM per device.

v0:
```python
import jax
import jax.numpy as jnp
from jax import lax
from jax.sharding import PartitionSpec as P


def group_size(slots):
    best = 1
    for cand in range(1, 9):
        if slots % cand == 0:
            best = cand
    return best


def accumulate(values, coords, count, panel, source_col, target_col, target_tiles, flipped):
    slots = values.shape[0]
    group = group_size(slots)
    tile = values.shape[1]
    width = panel.shape[2]
    offsets = jnp.arange(group, dtype=jnp.int32)

    def step(k, total):
        first = k * group
        vals = lax.dynamic_slice_in_dim(values, first, group, 0)
        cds = lax.dynamic_slice_in_dim(coords, first, group, 0)
        live = (first + offsets < count).astype(jnp.float32)
        picked = panel[cds[:, source_col]]
        if flipped:
            prod = jnp.einsum("tab,taf->tbf", vals, picked, preferred_element_type=jnp.float32)
        else:
            prod = jnp.einsum("tab,tbf->taf", vals, picked, preferred_element_type=jnp.float32)
        return total.at[cds[:, target_col]].add(prod * live[:, None, None])

    start = jnp.zeros((target_tiles, tile, width), jnp.float32)
    upper = slots // group
    return lax.fori_loop(0, upper, step, start)


def activate(v):
    return jax.nn.gelu(v, approximate=True)


def dense_step(summed, weight, cot_rows):
    pre = jnp.dot(summed, weight, preferred_element_type=jnp.float32)
    out, back = jax.vjp(activate, pre)
    grad_pre = back(cot_rows.astype(jnp.float32))[0].astype(jnp.bfloat16)
    terms = lax.dot_general(
        summed, grad_pre, (((0,), (0,)), ((), ())), preferred_element_type=jnp.float32
    )
    grad_summed = lax.dot_general(
        grad_pre, weight, (((1,), (1,)), ((), ())), preferred_element_type=jnp.float32
    ).astype(jnp.bfloat16)
    return (out.astype(jnp.bfloat16), terms, grad_summed)


def body(features, weight, cotangent, tile_values, tile_coords, tile_count):
    values = tile_values[0, 0]
    coords = tile_coords[0, 0]
    count = tile_count[0, 0]
    tile = values.shape[-1]
    width = weight.shape[0]
    nodes = cotangent.shape[0]
    row_tiles = nodes * lax.axis_size("col") // tile
    col_tiles = features.shape[0] // tile
    panel = lax.all_gather(features, "row", axis=1, tiled=True).reshape(col_tiles, tile, width)
    partial_value = accumulate(values, coords, count, panel, 1, 0, row_tiles, False)
    partial_value = partial_value.reshape(row_tiles * tile, width)
    totals = lax.psum_scatter(
        partial_value.astype(jnp.bfloat16), "col", scatter_dimension=0, tiled=True
    )
    activations, terms, grad_own = dense_step(totals, weight, cotangent)
    grad_weight = lax.psum(terms, ("row", "col"))
    grad_block = lax.all_gather(grad_own, "col", axis=0, tiled=True)
    back_panel = grad_block.reshape(row_tiles, tile, width)
    partial_back = accumulate(values, coords, count, back_panel, 0, 1, col_tiles, True)
    partial_back = partial_back.reshape(col_tiles * tile, width)
    grad_features = lax.psum_scatter(
        partial_back.astype(jnp.bfloat16), "row", scatter_dimension=1, tiled=True
    )
    return (activations, grad_features, grad_weight)


def solution(mesh):
    placed = (
        P("col", "row"),
        P(),
        P(("row", "col"), None),
        P("row", "col", None, None, None),
        P("row", "col", None, None),
        P("row", "col"),
    )
    return jax.shard_map(
        body,
        mesh=mesh,
        in_specs=placed,
        out_specs=(P(("row", "col"), None), P("col", "row"), P()),
        check_vma=False,
    )
```

profile of v0, /device:TPU:6, one launch (start us, length us, event | category | flops | bytes accessed | tf_op | source)
XLA Modules:
  0.0 781.0 jit_solution(11467857817144032404)
XLA Ops:
  8.0 48.7 %all-gather.3.cloned.1.call-done = bf16[2048,256]{0,1:T(8,128)(2,1)} async-done(((bf16[2048,16]{0,1:T(8,128)(2,1)}), bf16[2048,256]{0,1:T(8,128)(2,1)}) %all-gather.3.cloned.1.call-update) | async-done | bytes 1048592 | tf_op jit(solution)/shard_map/all_gather | solution.py:65
  60.6 71.0 %while.28 = (s32[]{:T(128)}, f32[32,128,256]{2,1,0:T(8,128)}, s32[96,2]{0,1:T(2,128)S(1)}, bf16[96,128,128]{2,1,0:T(8,128)(2,1)}, bf16[16,128,256]{2,1,0:T(8,128...) while((s32[]{:T(128)}, f32[32,128,256]{2,1,0:T(8,128)}, ...), condition=%wide.region_2.0_spmd.clone, body=%wide.region_0.0_spmd.clone.sunk | while | flops 67634256 | bytes 6033995 | solution.py:36
  63.2 3.4 scatter_fusion
  69.1 3.3 scatter_fusion
  75.1 3.3 scatter_fusion
  80.9 3.4 scatter_fusion
  86.9 3.4 scatter_fusion
  92.8 3.3 scatter_fusion
  98.7 3.3 scatter_fusion
  104.6 3.3 scatter_fusion
  110.5 3.4 scatter_fusion
  116.4 3.3 scatter_fusion
  122.4 3.3 scatter_fusion
  128.3 3.3 scatter_fusion
  131.6 3.8 convert_element_type.46
  135.6 218.8 %reduce-scatter.3.cloned.1.call-done = bf16[128,256]{1,0:T(8,128)(2,1)} async-done(((bf16[4096,256]{1,0:T(8,128)(2,1)}), bf16[128,256]{1,0:T(8,128)(2,1)}) %reduce-scatter.3.cloned.1.call-update) | async-done | bytes 65552 | tf_op jit(solution)/shard_map/reduce_scatter | solution.py:68
  360.8 79.3 %all-gather.5.cloned.1.call-done = bf16[4096,256]{1,0:T(8,128)(2,1)} async-done(((bf16[128,256]{1,0:T(8,128)(2,1)}), bf16[4096,256]{1,0:T(8,128)(2,1)}) %all-gather.5.cloned.1.call-update) | async-done | bytes 2097168 | tf_op jit(solution)/shard_map/all_gather | solution.py:73
  441.6 89.6 %while.29 = (s32[]{:T(128)}, f32[16,128,256]{2,1,0:T(8,128)}, s32[96,2]{0,1:T(2,128)S(1)}, bf16[96,128,128]{1,2,0:T(8,128)(2,1)}, bf16[32,128,256]{2,1,0:T(8,128...) while((s32[]{:T(128)}, f32[16,128,256]{2,1,0:T(8,128)}, ...), condition=%wide.region_6.7_spmd.clone, body=%wide.region_4.6_spmd.clone.sunk | while | flops 67634256 | bytes 6033995 | solution.py:36
  468.0 3.3 scatter_fusion.1
  475.5 3.3 scatter_fusion.1
  483.1 3.3 scatter_fusion.1
  498.0 3.4 scatter_fusion.1
  534.3 176.6 %all-reduce.2.cloned.1.call-done = f32[256,256]{1,0:T(8,128)} async-done(((f32[256,256]{1,0:T(8,128)}), f32[256,256]{1,0:T(8,128)}) %all-reduce.2.cloned.1.call-update) | async-done | bytes 262160 | tf_op jit(solution)/shard_map/psum | solution.py:72
  710.9 61.9 %reduce-scatter.5.cloned.1.call-done = bf16[2048,16]{0,1:T(8,128)(2,1)} async-done(((bf16[2048,256]{0,1:T(8,128)(2,1)}), bf16[2048,16]{0,1:T(8,128)(2,1)}) %reduce-scatter.5.cloned.1.call-update) | async-done | bytes 65552 | tf_op jit(solution)/shard_map/reduce_scatter | solution.py:77
  (182 shorter events, 124.1 us)
Async XLA Ops:
  7.2 347.1 %copy-start = (bf16[256,256]{1,0:T(8,128)(2,1)S(1)}, bf16[256,256]{1,0:T(8,128)(2,1)}, u32[]{:S(2)}) copy-start(bf16[256,256]{1,0:T(8,128)(2,1)} %param.11) | copy-start | bytes 393220
  7.2 49.5 %all-gather.3.cloned.1.call-start = ((), (), s32[]{:S(2)}) async-start(), calls=%async_computation.2 | async-start | bytes 1114112 | tf_op jit(solution)/shard_map/all_gather | solution.py:65
  7.9 346.4 %reduce-scatter.3.cloned.1.call-start = ((), (), s32[]{:S(2)}) async-start(), calls=%async_computation.3 | async-start | bytes 2162688 | tf_op jit(solution)/shard_map/reduce_scatter | solution.py:68
  8.0 52.7 %copy-start.2 = (s32[1,1,96,2]{2,3,1,0:T(2,128)S(1)}, s32[1,1,96,2]{2,3,1,0:T(2,128)}, u32[]{:S(2)}) copy-start(s32[1,1,96,2]{2,3,1,0:T(2,128)} %param.14) | copy-start | bytes 2308
  131.6 222.7 %copy-start.4 = (bf16[128,256]{1,0:T(8,128)(2,1)S(1)}, bf16[128,256]{1,0:T(8,128)(2,1)}, u32[]{:S(2)}) copy-start(bf16[128,256]{1,0:T(8,128)(2,1)} %param.12) | copy-start | bytes 196612
  135.5 221.5 %copy-start.1 = (bf16[96,128,128]{2,1,0:T(8,128)(2,1)S(1)}, bf16[96,128,128]{2,1,0:T(8,128)(2,1)}, u32[]{:S(2)}) copy-start(bf16[96,128,128]{2,1,0:T(8,128)(2,1)} %get-tuple-element.469) | copy-start | bytes 9437188
  135.5 304.5 %all-gather.5.cloned.1.call-start = ((), (), s32[]{:S(2)}) async-start(), calls=%async_computation.4 | async-start | bytes 2162688 | tf_op jit(solution)/shard_map/all_gather | solution.py:73
  356.9 354.0 %all-reduce.2.cloned.1.call-start = ((), (), s32[]{:S(2)}) async-start(), calls=%async_computation.6 | async-start | bytes 524288 | tf_op jit(solution)/shard_map/psum | solution.py:72
  356.9 2.8 copy-start.3
  360.7 412.1 %reduce-scatter.5.cloned.1.call-start = ((), (), s32[]{:S(2)}) async-start(), calls=%async_computation.5 | async-start | bytes 1114112 | tf_op jit(solution)/shard_map/reduce_scatter | solution.py:77
Sparse Core Ops, SparseCore 0:
  10.1 46.5 all-gather.2
  135.6 218.6 reduce-scatter.2
  358.5 81.4 all-gather.4
  446.2 264.6 all-reduce.1
  714.2 58.6 reduce-scatter.4
where the time goes:
time: 783 us; the launch traced here: 781 us
  waiting for transfers between devices  586 us (75%)
  other arithmetic  101 us (13%)
  local copies, waits for them, and re-layouts  46.1 us (6%)
  matrix products  33.2 us (4%)
  between operations  13.8 us (2%)
    reduce_scatter x1, waiting for transfers between devices, body(): lax.psum_scatter(partial_value.astype(jnp.bfloat16), 'col', scatter_dimen...  219 us
    psum x1, waiting for transfers between devices, body(): grad_weight = lax.psum(terms, ('row', 'col'))  177 us
    scatter-add x24, other arithmetic, step(): return total.at[cds[:, target_col]].add(prod * live[:, None, None])  79.6 us
    all_gather x1, waiting for transfers between devices, body(): grad_block = lax.all_gather(grad_own, 'col', axis=0, tiled=True)  79.3 us
    reduce_scatter x1, waiting for transfers between devices, body(): lax.psum_scatter(partial_back.astype(jnp.bfloat16), 'row', scatter_dimens...  61.9 us
    all_gather x1, waiting for transfers between devices, body(): lax.all_gather(features, 'row', axis=1, tiled=True)  48.7 us
    gather x24, local copies, waits for them, and re-layouts, step(): picked = panel[cds[:, source_col]]  33 us
  transfers between devices with their start and end apart: 5, of which 5 were waited for; matrix products, arithmetic and copies ran while one was open for 13% of the time, Pallas kernels for 0%

commit v1 on v0

v1 whole, which is shorter than its diff:
```python
import jax
import jax.numpy as jnp
from jax import lax
from jax.experimental import pallas as pl
from jax.experimental.pallas import tpu as pltpu
from jax.sharding import Mesh, PartitionSpec as P

BF = jnp.bfloat16
F32 = jnp.float32
SMEM = pl.BlockSpec(memory_space=pltpu.SMEM)
VMEM = pl.BlockSpec(memory_space=pltpu.VMEM)
AXES = ("z", "core", "y", "x")
NZ, NC, NY, NX = 8, 2, 8, 4
NL = 2
NH = NY // NL
NEAR = NL * NX
SHARE = 16
TERMS = 64
UNROLL = 8


def device(z, core, y, x):
    return ((z * NC + core) * NY + y) * NX + x


def turned(i, core, n):
    return i if core == 0 else (n - i) % n


def near_groups():
    return [
        [device(z, core, h * NL + d // NX, d % NX) for d in range(NEAR)]
        for z in range(NZ)
        for core in range(NC)
        for h in range(NH)
    ]


def far_groups():
    return [
        [device(z, core, turned(h, core, NH) * NL + d // NX, d % NX) for h in range(NH)]
        for z in range(NZ)
        for core in range(NC)
        for d in range(NEAR)
    ]


def depth_groups():
    return [
        [device(turned(z, core, NZ), core, y, x) for z in range(NZ)]
        for core in range(NC)
        for y in range(NY)
        for x in range(NX)
    ]


def exchange(x, groups):
    return lax.all_to_all(x, AXES, 0, 0, axis_index_groups=groups, tiled=True)


def place(i, core, n):
    return jnp.where(core == 0, i, (n - i) % n)


def forward_kernel(coords, info, own, other, vals, out, panel, acc):
    tile = vals.shape[1]
    count, core = info[0], info[1]
    for b in range(panel.shape[0] // tile):
        cols = slice(b * tile, (b + 1) * tile)
        for part, owner in ((own, core), (other, 1 - core)):
            slab = jnp.concatenate([part[place(z, owner, NZ), :, cols] for z in range(NZ)], axis=0)
            at = pl.multiple_of(owner * tile, tile)
            panel[cols, pl.ds(at, tile)] = slab.T
    acc[...] = jnp.zeros_like(acc)

    def step(g, carry):
        prods = []
        for u in range(UNROLL):
            s = g * UNROLL + u
            c = pl.multiple_of(coords[2 * s + 1] * tile, tile)
            prods.append(jnp.dot(vals[s], panel[pl.ds(c, tile), :], preferred_element_type=F32))
        for u in range(UNROLL):
            r = coords[2 * (g * UNROLL + u)]
            acc[r] += prods[u]
        return carry

    lax.fori_loop(0, (count + UNROLL - 1) // UNROLL, step, 0)
    for h in range(NH):
        at = place(h, core, NH)
        for d in range(NEAR):
            out[d, at] = acc[h * NEAR + d].astype(BF)


def add_kernel(parts, out):
    out[...] = jnp.sum(parts[...].astype(F32), axis=0).astype(BF)


def dense_kernel(info, parts, weight, cot, act, sent, scratch):
    core = info[1]
    width = weight.shape[0]
    order = [(2 * z + c) * SHARE for c in range(NC) for z in range(NZ)]
    s = jnp.sum(parts[...].astype(F32), axis=0).astype(BF)
    w = jnp.concatenate([weight[a : a + SHARE, :] for a in order], axis=0)
    v = jnp.dot(s, w, preferred_element_type=F32)
    k = 0.7978845608028654
    t = jnp.tanh(k * (v + 0.044715 * (v * v * v)))
    act[...] = (0.5 * v * (1.0 + t)).astype(BF)
    slope = 0.5 * (1.0 + t) + 0.5 * v * (1.0 - t * t) * (k * (1.0 + 3.0 * 0.044715 * v * v))
    g = (cot[...].astype(F32) * slope).astype(BF)
    back = lax.dot_general(w, g, (((1,), (1,)), ((), ())), preferred_element_type=F32).astype(BF)
    terms = lax.dot_general(s, g, (((0,), (0,)), ((), ())), preferred_element_type=F32)
    for i, a in enumerate(order):
        scratch[a : a + SHARE, :] = terms[i * SHARE : (i + 1) * SHARE, :]
    half = back.shape[1]
    rows = width // NH
    for h in range(NH):
        at = place(h, core, NH)
        sent[at, :width, :] = back
        sent[at, width : width + rows, :] = scratch[rows * h : rows * (h + 1), :half].astype(BF)
        sent[at, width + rows :, :] = scratch[rows * h : rows * (h + 1), half:].astype(BF)


def spread_kernel(got, sent):
    width = got.shape[1] - 2 * TERMS
    terms = jnp.sum(got[:, width:, :].astype(F32), axis=0)
    for d in range(NEAR):
        for h in range(NH):
            sent[d, h * width : (h + 1) * width, :] = got[h, :width, :]
        piece = jnp.concatenate([terms[8 * d : 8 * d + 8], terms[TERMS + 8 * d : TERMS + 8 * d + 8]], axis=0)
        sent[d, NH * width :, :] = piece.astype(BF)


def backward_kernel(coords, info, panel, vals, mine, theirs, acc):
    count, core = info[0], info[1]
    tiles, width, tile = acc.shape
    acc[...] = jnp.zeros_like(acc)

    def step(g, carry):
        prods = []
        for u in range(UNROLL):
            s = g * UNROLL + u
            r = coords[2 * s]
            h = pl.multiple_of(place(lax.div(r, NEAR), core, NH) * width, width)
            prods.append(jnp.dot(panel[lax.rem(r, NEAR), pl.ds(h, width), :], vals[s], preferred_element_type=F32))
        for u in range(UNROLL):
            c = coords[2 * (g * UNROLL + u) + 1]
            acc[c] += prods[u]
        return carry

    lax.fori_loop(0, (count + UNROLL - 1) // UNROLL, step, 0)
    terms = jnp.sum(panel[:, NH * width :, :].astype(F32), axis=0).astype(BF)
    for out, owner in ((mine, core), (theirs, 1 - core)):
        for z in range(NZ):
            a = pl.multiple_of(owner * tile + z * SHARE, SHARE)
            at = place(z, owner, NZ)
            for c in range(tiles):
                out[at, SHARE * c : SHARE * (c + 1), :] = acc[c, pl.ds(a, SHARE), :].astype(BF)
            out[at, SHARE * tiles :, :] = terms


def params(mib):
    return pltpu.CompilerParams(vmem_limit_bytes=mib * 1024 * 1024)


def body(features, weight, cotangent, tile_values, tile_coords, tile_count):
    coords = tile_coords.reshape(-1)
    core = lax.axis_index("core").astype(jnp.int32)
    nodes, share = features.shape
    slots, tile = tile_values.shape[2:4]
    width = weight.shape[0]
    row_tiles = NY * NX
    col_tiles = nodes // tile
    swap = ((0, 1), (1, 0))

    own = jnp.broadcast_to(features.T[None], (NZ, share, nodes))
    own = exchange(own, depth_groups())
    own, count = lax.optimization_barrier((own, tile_count[0, 0]))
    other = lax.ppermute(own, "core", swap)
    live = lax.broadcasted_iota(jnp.int32, (slots, tile, tile), 0) < count
    vals = jnp.where(live, tile_values[0, 0], jnp.zeros((), BF))
    info = jnp.stack([count, core])
    sums = pl.pallas_call(
        forward_kernel,
        out_shape=jax.ShapeDtypeStruct((NEAR, NH, tile, width), BF),
        in_specs=[SMEM, SMEM, VMEM, VMEM, VMEM],
        out_specs=VMEM,
        scratch_shapes=[pltpu.VMEM((nodes, width), BF), pltpu.VMEM((row_tiles, tile, width), F32)],
        compiler_params=params(24),
        name="forward_tiles",
    )(coords, info, own, other, vals)
    parts = exchange(sums, near_groups())
    parts = pl.pallas_call(
        add_kernel,
        out_shape=jax.ShapeDtypeStruct((NH, tile, width), BF),
        in_specs=[VMEM],
        out_specs=VMEM,
        compiler_params=params(24),
        name="add_near",
    )(parts)
    parts = exchange(parts, far_groups())
    activations, sent = pl.pallas_call(
        dense_kernel,
        out_shape=(
            jax.ShapeDtypeStruct((tile, width), BF),
            jax.ShapeDtypeStruct((NH, width + 2 * TERMS, tile), BF),
        ),
        in_specs=[SMEM, VMEM, VMEM, VMEM],
        out_specs=(VMEM, VMEM),
        scratch_shapes=[pltpu.VMEM((width, width), F32)],
        compiler_params=params(24),
        name="dense",
    )(info, parts, weight, cotangent)
    got = exchange(sent, far_groups())
    sent = pl.pallas_call(
        spread_kernel,
        out_shape=jax.ShapeDtypeStruct((NEAR, NH * width + 16, tile), BF),
        in_specs=[VMEM],
        out_specs=VMEM,
        compiler_params=params(24),
        name="spread_near",
    )(got)
    panel = exchange(sent, near_groups())
    mine, theirs = pl.pallas_call(
        backward_kernel,
        out_shape=(jax.ShapeDtypeStruct((NZ, width + 16, tile), BF),) * 2,
        in_specs=[SMEM, SMEM, VMEM, VMEM],
        out_specs=(VMEM, VMEM),
        scratch_shapes=[pltpu.VMEM((col_tiles, width, tile), F32)],
        compiler_params=params(24),
        name="backward_tiles",
    )(coords, info, panel, vals)
    got = lax.ppermute(theirs, "core", swap)
    both = (mine.astype(F32) + got.astype(F32)).astype(BF)
    back = exchange(both, depth_groups())
    back = jnp.sum(back.astype(F32), axis=0)
    piece = back[width:]
    grad_features = back[:width].astype(BF).reshape(col_tiles, share, tile)
    grad_features = grad_features.transpose(0, 2, 1).reshape(nodes, share)
    whole = jnp.broadcast_to(piece[None], (row_tiles,) + piece.shape)
    whole = lax.all_to_all(whole, ("y", "x"), 0, 0, tiled=True)
    grad_weight = whole.reshape(row_tiles, 2, 8, tile).transpose(0, 2, 1, 3).reshape(width, width)
    return (activations, grad_features, grad_weight)


def solution(mesh):
    fine = Mesh(mesh.devices.reshape(NZ, NC, NY, NX), AXES)
    row, col = AXES[:2], AXES[2:]
    placed = (
        P(col, row),
        P(),
        P(row + col, None),
        P(row, col, None, None, None),
        P(row, col, None, None),
        P(row, col),
    )
    return jax.shard_map(
        body,
        mesh=fine,
        in_specs=placed,
        out_specs=(P(row + col, None), P(col, row), P()),
        check_vma=False,
    )
```

time: 783 us -> 182 us (0.23)
  waiting for transfers between devices: 586 us -> 27.4 us
  blocking collectives: 0 us -> 117 us
  other arithmetic: 101 us -> 2.47 us
  local copies, waits for them, and re-layouts: 46.1 us -> 4.67 us
  matrix products: 33.2 us -> 0 us
  starting transfers between devices: 0.2 us -> 22.6 us
  between operations: 13.8 us -> 1.38 us
    reduce_scatter x2 -> x0, waiting for transfers between devices: 281 us -> none  [the longest x1 219 us: body(): lax.psum_scatter(partial_value.astype(jnp.bfloat16), 'col', scatter_dimen...]
    psum x1 -> x0, waiting for transfers between devices: 177 us -> none  [body(): grad_weight = lax.psum(terms, ('row', 'col'))]
    all_gather x2 -> x0, waiting for transfers between devices: 128 us -> none  [the longest x1 79.3 us: body(): grad_block = lax.all_gather(grad_own, 'col', axis=0, tiled=True)]
    all_to_all x0 -> x5, blocking collectives: none -> 117 us  [exchange(): return lax.all_to_all(x, AXES, 0, 0, axis_index_groups=groups, tiled=True)]
    scatter-add x24 -> x0, other arithmetic: 79.6 us -> none  [step(): return total.at[cds[:, target_col]].add(prod * live[:, None, None])]
    dot_general x27 -> x0, matrix products: 33.2 us -> none  [the longest x12 14.9 us: step(): jnp.einsum('tab,taf->tbf', vals, picked, preferred_element_type=jnp.float32)]
    gather x24 -> x0, local copies, waits for them, and re-layouts: 33 us -> none  [step(): picked = panel[cds[:, source_col]]]
    all_to_all x0 -> x2, waiting for transfers between devices: none -> 25.4 us  [the longest x1 16.1 us: exchange(): return lax.all_to_all(x, AXES, 0, 0, axis_index_groups=groups, tiled=True)]
  transfers between devices with their start and end apart: 5 -> 4, of which waited for: 5 -> 3; matrix products, arithmetic and copies ran while one was open for 13% -> 2% of each run, Pallas kernels for 0% -> 0%
where the time goes in v1:
time: 182 us; the launch traced here: 181 us
  blocking collectives  117 us (64%)
  waiting for transfers between devices  27.4 us (15%)
  starting transfers between devices  22.6 us (12%)
  Pallas kernels  5.92 us (3%)
  local copies, waits for them, and re-layouts  4.67 us (3%)
  other arithmetic  2.47 us (1%)
    all_to_all x5, blocking collectives, exchange(): return lax.all_to_all(x, AXES, 0, 0, axis_index_groups=groups, tiled=True)  117 us
    all_to_all x1, waiting for transfers between devices, exchange(): return lax.all_to_all(x, AXES, 0, 0, axis_index_groups=groups, tiled=True)  16.1 us
    all_to_all x1, starting transfers between devices, exchange(): return lax.all_to_all(x, AXES, 0, 0, axis_index_groups=groups, tiled=True)  10.3 us
    all_to_all x1, waiting for transfers between devices, body(): whole = lax.all_to_all(whole, ('y', 'x'), 0, 0, tiled=True)  9.29 us
    all_to_all x1, starting transfers between devices, body(): whole = lax.all_to_all(whole, ('y', 'x'), 0, 0, tiled=True)  8.46 us
  transfers between devices with their start and end apart: 4, of which 3 were waited for; matrix products, arithmetic and copies ran while one was open for 2% of the time, Pallas kernels for 0%

profile of v1, /device:TPU:6, one launch (start us, length us, event | category | flops | bytes accessed | tf_op | source)
XLA Modules:
  0.0 181.0 jit_solution(9159579581261698889)
XLA Ops:
  0.6 1.7 broadcast_in_dim.8
  2.3 10.3 %all-to-all-start = ((bf16[8,16,2048]{2,1,0:T(8,128)(2,1)}), bf16[8,16,2048]{2,1,0:T(8,128)(2,1)S(1)}, u32[]{:S(2)}, u32[]{:S(2)}) async-start(bf16[8,16,2048]{2,1,0:T(8,128)(2,1)} %broadcast_in_dim.8), calls=%async_computation | async-start | bytes 1048576 | tf_op jit(solution)/shard_map/all_to_all | solution.py:58
  13.3 16.1 %all-to-all-done.own = bf16[8,16,2048]{2,1,0:T(8,128)(2,1)S(1)} async-done(((bf16[8,16,2048]{2,1,0:T(8,128)(2,1)}), bf16[8,16,2048]{2,1,0:T(8,128)(2,1)S(1)}, u32[]{:S(2)}, u32[]{:S(2)}) %all-to-all-start) | async-done | bytes 524320 | tf_op jit(solution)/shard_map/all_to_all | solution.py:58
  29.4 1.9 %collective-permute-start = (bf16[8,16,2048]{2,1,0:T(8,128)(2,1)S(1)}, bf16[8,16,2048]{2,1,0:T(8,128)(2,1)S(1)}, u32[]{:S(2)}, u32[]{:S(2)}) collective-permute-start(bf16[8,16,2048]{2,1,0:T(8,128)(2,1)S(1)} %all-to-all-done.own), channel_id=1, source_target_pairs={{0,32},{32,0},{1,33},{33,1},{2,34},{34,2},{3,35},{35,3},{4,36},{36... | collective-permute-start | bytes 1572872 | tf_op jit(solution)/shard_map/ppermute | solution.py:178
  31.4 0.8 copy.10
  32.3 2.2 %bitcast_select_fusion.vals = bf16[96,128,128]{2,1,0:T(8,128)(2,1)S(1)} fusion(bf16[1,1,96,128,128]{4,3,2,1,0:T(8,128)(2,1)} %param.9, pred[96]{0:T(512)(128)(4,1)S(1)} %iota_compare_fusion), kind=kLoop, calls=%fused_computation | loop fusion | flops 1572864 | bytes 6291552 | tf_op jit(solution)/shard_map/jit(_where)/select_n | solution.py:180
  34.5 2.2 %forward_tiles.1 = bf16[8,4,128,256]{3,2,1,0:T(8,128)(2,1)S(1)} custom-call(s32[192]{0:T(256)S(1)} %reshape.23.coords, s32[2]{0:T(128)S(1)} %pad_add_fusion.info, bf16[8,16,2048]{2,1,0:T(8,128)(2,1)S(1)} %all-to-all-done.own, bf16[8,16,2048]{2,1,0:T(8,128)(2,1)S(1)} %collective-permute-done.other, bf16[96,128,128]{2,1,0:T(8,128)(2,1)S(1)} %bitcast_select_fusion.vals), custom_call_target="tpu_custom_call" | custom-call | tf_op jit(solution)/shard_map/forward_tiles/pallas_call | solution.py:182
  36.8 31.4 %all_to_all.35.parts = bf16[8,4,128,256]{3,2,1,0:T(8,128)(2,1)S(1)} all-to-all(bf16[8,4,128,256]{3,2,1,0:T(8,128)(2,1)S(1)} %forward_tiles.1), channel_id=1, replica_groups={{0,1,2,3,4,5,6,7},{8,9,10,11,12,13,14,15},{16,17,18,19,20,21,22,23},{24..., dimensions={0} | all-to-all | bytes 4194304 | tf_op jit(solution)/shard_map/all_to_all | solution.py:58
  68.2 0.3 add_near.1
  68.5 16.7 %all_to_all.36.parts = bf16[4,128,256]{2,1,0:T(8,128)(2,1)S(1)} all-to-all(bf16[4,128,256]{2,1,0:T(8,128)(2,1)S(1)} %add_near.1), channel_id=1, replica_groups={{0,8,16,24},{1,9,17,25},{2,10,18,26},{3,11,19,27},{4,12,20,28},{5,13,21..., dimensions={0} | all-to-all | bytes 524288 | tf_op jit(solution)/shard_map/all_to_all | solution.py:58
  85.2 1.4 dense.1
  86.6 15.9 %all_to_all.37.got = bf16[4,384,128]{2,1,0:T(8,128)(2,1)S(1)} all-to-all(bf16[4,384,128]{2,1,0:T(8,128)(2,1)S(1)} %get-tuple-element.12), channel_id=1, replica_groups={{0,8,16,24},{1,9,17,25},{2,10,18,26},{3,11,19,27},{4,12,20,28},{5,13,21..., dimensions={0} | all-to-all | bytes 786432 | tf_op jit(solution)/shard_map/all_to_all | solution.py:58
  102.5 0.3 spread_near.1
  102.8 28.8 %all_to_all.38.panel = bf16[8,1040,128]{2,1,0:T(8,128)(2,1)S(1)} all-to-all(bf16[8,1040,128]{2,1,0:T(8,128)(2,1)S(1)} %spread_near.1), channel_id=1, replica_groups={{0,1,2,3,4,5,6,7},{8,9,10,11,12,13,14,15},{16,17,18,19,20,21,22,23},{24..., dimensions={0} | all-to-all | bytes 4259840 | tf_op jit(solution)/shard_map/all_to_all | solution.py:58
  131.5 1.7 backward_tiles.1
  133.3 1.9 %collective-permute-start.1 = (bf16[8,272,128]{2,1,0:T(8,128)(2,1)S(1)}, bf16[8,272,128]{2,1,0:T(8,128)(2,1)S(1)}, u32[]{:S(2)}, u32[]{:S(2)}) collective-permute-start(bf16[8,272,128]{2,1,0:T(8,128)(2,1)S(1)} %get-tuple-element.14), channel_id=1, source_target_pairs={{0,32},{32,0},{1,33},{33,1},{2,34},{34,2},{3,35},{35,3},{4,36},{36... | collective-permute-start | bytes 1671176 | tf_op jit(solution)/shard_map/ppermute | solution.py:232
  135.2 1.9 %collective-permute-done.1 = bf16[8,272,128]{2,1,0:T(8,128)(2,1)S(1)} collective-permute-done((bf16[8,272,128]{2,1,0:T(8,128)(2,1)S(1)}, bf16[8,272,128]{2,1,0:T(8,128)(2,1)S(1)}, u32[]{:S(2)}, u32[]{:S(2)}) %collective-permute-start.1) | collective-permute-done | bytes 557088 | tf_op jit(solution)/shard_map/ppermute | solution.py:232
  137.1 0.1 add_convert_fusion
  137.3 23.8 %all_to_all.39 = bf16[8,272,128]{2,1,0:T(8,128)(2,1)S(1)} all-to-all(bf16[8,272,128]{2,1,0:T(8,128)(2,1)S(1)} %add_convert_fusion), channel_id=1, replica_groups={{0,64,128,192,256,320,384,448},{1,65,129,193,257,321,385,449},{2,66,130..., dimensions={0} | all-to-all | bytes 1114112 | tf_op jit(solution)/shard_map/all_to_all | solution.py:58
  161.2 0.7 broadcast_in_dim.18
  161.9 8.5 %all-to-all-start.6 = ((f32[32,16,128]{2,1,0:T(8,128)}), f32[32,16,128]{2,1,0:T(8,128)S(1)}, u32[]{:S(2)}, u32[]{:S(2)}) async-start(f32[32,16,128]{2,1,0:T(8,128)} %broadcast_in_dim.18), calls=%async_computation.6 | async-start | bytes 524288 | tf_op jit(solution)/shard_map/all_to_all | solution.py:240
  170.4 0.6 copy.14
  171.0 9.3 %all-to-all-done.6 = f32[32,16,128]{2,1,0:T(8,128)S(1)} async-done(((f32[32,16,128]{2,1,0:T(8,128)}), f32[32,16,128]{2,1,0:T(8,128)S(1)}, u32[]{:S(2)}, u32[]{:S(2)}) %all-to-all-start.6) | async-done | bytes 262176 | tf_op jit(solution)/shard_map/all_to_all | solution.py:240
  180.3 0.7 copy.17
  (11 shorter events, 0.3 us)
Async XLA Ops:
  2.3 27.1 %all-to-all-start = ((bf16[8,16,2048]{2,1,0:T(8,128)(2,1)}), bf16[8,16,2048]{2,1,0:T(8,128)(2,1)S(1)}, u32[]{:S(2)}, u32[]{:S(2)}) async-start(bf16[8,16,2048]{2,1,0:T(8,128)(2,1)} %broadcast_in_dim.8), calls=%async_computation | async-start | bytes 1048576 | tf_op jit(solution)/shard_map/all_to_all | solution.py:58
  29.4 5.1 %collective-permute-start = (bf16[8,16,2048]{2,1,0:T(8,128)(2,1)S(1)}, bf16[8,16,2048]{2,1,0:T(8,128)(2,1)S(1)}, u32[]{:S(2)}, u32[]{:S(2)}) collective-permute-start(bf16[8,16,2048]{2,1,0:T(8,128)(2,1)S(1)} %all-to-all-done.own), channel_id=1, source_target_pairs={{0,32},{32,0},{1,33},{33,1},{2,34},{34,2},{3,35},{35,3},{4,36},{36... | collective-permute-start | bytes 1572872 | tf_op jit(solution)/shard_map/ppermute | solution.py:178
  68.2 17.0 %copy-start = (bf16[256,256]{1,0:T(8,128)(2,1)S(1)}, bf16[256,256]{1,0:T(8,128)(2,1)}, u32[]{:S(2)}) copy-start(bf16[256,256]{1,0:T(8,128)(2,1)} %weight.1) | copy-start | bytes 393220
  68.2 17.0 %copy-start.1 = (bf16[128,256]{1,0:T(8,128)(2,1)S(1)}, bf16[128,256]{1,0:T(8,128)(2,1)}, u32[]{:S(2)}) copy-start(bf16[128,256]{1,0:T(8,128)(2,1)} %cot.1) | copy-start | bytes 196612
  133.3 3.9 %collective-permute-start.1 = (bf16[8,272,128]{2,1,0:T(8,128)(2,1)S(1)}, bf16[8,272,128]{2,1,0:T(8,128)(2,1)S(1)}, u32[]{:S(2)}, u32[]{:S(2)}) collective-permute-start(bf16[8,272,128]{2,1,0:T(8,128)(2,1)S(1)} %get-tuple-element.14), channel_id=1, source_target_pairs={{0,32},{32,0},{1,33},{33,1},{2,34},{34,2},{3,35},{35,3},{4,36},{36... | collective-permute-start | bytes 1671176 | tf_op jit(solution)/shard_map/ppermute | solution.py:232
  161.9 18.4 %all-to-all-start.6 = ((f32[32,16,128]{2,1,0:T(8,128)}), f32[32,16,128]{2,1,0:T(8,128)S(1)}, u32[]{:S(2)}, u32[]{:S(2)}) async-start(f32[32,16,128]{2,1,0:T(8,128)} %broadcast_in_dim.18), calls=%async_computation.6 | async-start | bytes 524288 | tf_op jit(solution)/shard_map/all_to_all | solution.py:240

commit v2 on v1

--- a/solution.py
+++ b/solution.py
@@ -11,11 +11,10 @@
 VMEM = pl.BlockSpec(memory_space=pltpu.VMEM)
 AXES = ("z", "core", "y", "x")
 NZ, NC, NY, NX = 8, 2, 8, 4
-NL = 2
-NH = NY // NL
-NEAR = NL * NX
 SHARE = 16
-TERMS = 64
+QUAD = 4
+BLOCKS = NY * NX // QUAD
+TERMS = 2 * 32
 UNROLL = 8
 
 
@@ -27,21 +26,32 @@
     return i if core == 0 else (n - i) % n
 
 
-def near_groups():
+def quad(core, n, f):
+    y = (f // 2 * 2 + n // 2 + core) % NY
+    x = (f % 2 * 2 + n % 2 + core) % NX
+    return y * NX + x
+
+
+def spot_of(r, core):
+    y, x = (r // NX - core) % NY, (r % NX - core) % NX
+    return (y % 2 * 2 + x % 2) * BLOCKS + y // 2 * 2 + x // 2
+
+
+def quad_groups():
     return [
-        [device(z, core, h * NL + d // NX, d % NX) for d in range(NEAR)]
+        [device(z, core, *divmod(quad(core, n, f), NX)) for n in range(QUAD)]
         for z in range(NZ)
         for core in range(NC)
-        for h in range(NH)
+        for f in range(BLOCKS)
     ]
 
 
-def far_groups():
+def block_groups():
     return [
-        [device(z, core, turned(h, core, NH) * NL + d // NX, d % NX) for h in range(NH)]
+        [device(z, core, *divmod(quad(core, n, f), NX)) for f in range(BLOCKS)]
         for z in range(NZ)
         for core in range(NC)
-        for d in range(NEAR)
+        for n in range(QUAD)
     ]
 
 
@@ -85,17 +95,16 @@
         return carry
 
     lax.fori_loop(0, (count + UNROLL - 1) // UNROLL, step, 0)
-    for h in range(NH):
-        at = place(h, core, NH)
-        for d in range(NEAR):
-            out[d, at] = acc[h * NEAR + d].astype(BF)
+    for n in range(QUAD):
+        for f in range(BLOCKS):
+            out[n, f] = acc[n * BLOCKS + f].astype(BF)
 
 
 def add_kernel(parts, out):
     out[...] = jnp.sum(parts[...].astype(F32), axis=0).astype(BF)
 
 
-def dense_kernel(info, parts, weight, cot, act, sent, scratch):
+def dense_kernel(info, parts, weight, cot, act, grads, sent, scratch):
     core = info[1]
     width = weight.shape[0]
     order = [(2 * z + c) * SHARE for c in range(NC) for z in range(NZ)]
@@ -112,22 +121,29 @@
     for i, a in enumerate(order):
         scratch[a : a + SHARE, :] = terms[i * SHARE : (i + 1) * SHARE, :]
     half = back.shape[1]
-    rows = width // NH
-    for h in range(NH):
-        at = place(h, core, NH)
-        sent[at, :width, :] = back
-        sent[at, width : width + rows, :] = scratch[rows * h : rows * (h + 1), :half].astype(BF)
-        sent[at, width + rows :, :] = scratch[rows * h : rows * (h + 1), half:].astype(BF)
+    rows = width // NZ
+    grads[...] = back
+    for z in range(NZ):
+        at = place(z, core, NZ)
+        sent[at, :rows, :] = scratch[rows * z : rows * (z + 1), :half].astype(BF)
+        sent[at, rows:, :] = scratch[rows * z : rows * (z + 1), half:].astype(BF)
+
+
+def pack_kernel(grads, terms, sent):
+    width = grads.shape[0]
+    piece = jnp.sum(terms[...].astype(F32), axis=0).astype(BF)
+    for f in range(BLOCKS):
+        sent[f, :width, :] = grads[...]
+        sent[f, width:, :] = piece
 
 
 def spread_kernel(got, sent):
-    width = got.shape[1] - 2 * TERMS
-    terms = jnp.sum(got[:, width:, :].astype(F32), axis=0)
-    for d in range(NEAR):
-        for h in range(NH):
-            sent[d, h * width : (h + 1) * width, :] = got[h, :width, :]
-        piece = jnp.concatenate([terms[8 * d : 8 * d + 8], terms[TERMS + 8 * d : TERMS + 8 * d + 8]], axis=0)
-        sent[d, NH * width :, :] = piece.astype(BF)
+    width = got.shape[1] - TERMS
+    piece = jnp.sum(got[:, width:, :].astype(F32), axis=0).astype(BF)
+    for n in range(QUAD):
+        for f in range(BLOCKS):
+            sent[n, f * width : (f + 1) * width, :] = got[f, :width, :]
+        sent[n, BLOCKS * width :, :] = piece
 
 
 def backward_kernel(coords, info, panel, vals, mine, theirs, acc):
@@ -139,16 +155,16 @@
         prods = []
         for u in range(UNROLL):
             s = g * UNROLL + u
-            r = coords[2 * s]
-            h = pl.multiple_of(place(lax.div(r, NEAR), core, NH) * width, width)
-            prods.append(jnp.dot(panel[lax.rem(r, NEAR), pl.ds(h, width), :], vals[s], preferred_element_type=F32))
+            spot = coords[2 * s]
+            at = pl.multiple_of(lax.rem(spot, BLOCKS) * width, width)
+            prods.append(jnp.dot(panel[lax.div(spot, BLOCKS), pl.ds(at, width), :], vals[s], preferred_element_type=F32))
         for u in range(UNROLL):
             c = coords[2 * (g * UNROLL + u) + 1]
             acc[c] += prods[u]
         return carry
 
     lax.fori_loop(0, (count + UNROLL - 1) // UNROLL, step, 0)
-    terms = jnp.sum(panel[:, NH * width :, :].astype(F32), axis=0).astype(BF)
+    terms = jnp.sum(panel[:, BLOCKS * width :, :].astype(F32), axis=0).astype(BF)
     for out, owner in ((mine, core), (theirs, 1 - core)):
         for z in range(NZ):
             a = pl.multiple_of(owner * tile + z * SHARE, SHARE)
@@ -158,12 +174,25 @@
             out[at, SHARE * tiles :, :] = terms
 
 
+def finish_kernel(info, got, grads, weights):
+    core = info[1]
+    share, tile = SHARE, got.shape[2]
+    width = got.shape[1] - TERMS
+    rows = TERMS // 2
+    total = jnp.sum(got[:, :width, :].astype(F32), axis=0).astype(BF)
+    for c in range(width // share):
+        grads[:, c * tile : (c + 1) * tile] = total[c * share : (c + 1) * share, :]
+    for z in range(NZ):
+        at = place(z, core, NZ)
+        weights[rows * z : rows * (z + 1), :tile] = got[at, width : width + rows, :].astype(F32)
+        weights[rows * z : rows * (z + 1), tile:] = got[at, width + rows :, :].astype(F32)
+
+
 def params(mib):
     return pltpu.CompilerParams(vmem_limit_bytes=mib * 1024 * 1024)
 
 
 def body(features, weight, cotangent, tile_values, tile_coords, tile_count):
-    coords = tile_coords.reshape(-1)
     core = lax.axis_index("core").astype(jnp.int32)
     nodes, share = features.shape
     slots, tile = tile_values.shape[2:4]
@@ -174,55 +203,66 @@
 
     own = jnp.broadcast_to(features.T[None], (NZ, share, nodes))
     own = exchange(own, depth_groups())
-    own, count = lax.optimization_barrier((own, tile_count[0, 0]))
+    own, count, coords = lax.optimization_barrier((own, tile_count[0, 0], tile_coords))
+    coords = jnp.stack([spot_of(coords[0, 0, :, 0], core), coords[0, 0, :, 1]], axis=-1).reshape(-1)
     other = lax.ppermute(own, "core", swap)
     live = lax.broadcasted_iota(jnp.int32, (slots, tile, tile), 0) < count
     vals = jnp.where(live, tile_values[0, 0], jnp.zeros((), BF))
     info = jnp.stack([count, core])
     sums = pl.pallas_call(
         forward_kernel,
-        out_shape=jax.ShapeDtypeStruct((NEAR, NH, tile, width), BF),
+        out_shape=jax.ShapeDtypeStruct((QUAD, BLOCKS, tile, width), BF),
         in_specs=[SMEM, SMEM, VMEM, VMEM, VMEM],
         out_specs=VMEM,
         scratch_shapes=[pltpu.VMEM((nodes, width), BF), pltpu.VMEM((row_tiles, tile, width), F32)],
         compiler_params=params(24),
         name="forward_tiles",
     )(coords, info, own, other, vals)
-    parts = exchange(sums, near_groups())
+    parts = exchange(sums, quad_groups())
     parts = pl.pallas_call(
         add_kernel,
-        out_shape=jax.ShapeDtypeStruct((NH, tile, width), BF),
+        out_shape=jax.ShapeDtypeStruct((BLOCKS, tile, width), BF),
         in_specs=[VMEM],
         out_specs=VMEM,
         compiler_params=params(24),
-        name="add_near",
+        name="add_quad",
     )(parts)
-    parts = exchange(parts, far_groups())
-    activations, sent = pl.pallas_call(
+    parts = exchange(parts, block_groups())
+    activations, grads, terms = pl.pallas_call(
         dense_kernel,
         out_shape=(
             jax.ShapeDtypeStruct((tile, width), BF),
-            jax.ShapeDtypeStruct((NH, width + 2 * TERMS, tile), BF),
+            jax.ShapeDtypeStruct((width, tile), BF),
+            jax.ShapeDtypeStruct((NZ, TERMS, tile), BF),
         ),
         in_specs=[SMEM, VMEM, VMEM, VMEM],
-        out_specs=(VMEM, VMEM),
+        out_specs=(VMEM, VMEM, VMEM),
         scratch_shapes=[pltpu.VMEM((width, width), F32)],
         compiler_params=params(24),
         name="dense",
     )(info, parts, weight, cotangent)
-    got = exchange(sent, far_groups())
+    terms = exchange(terms, depth_groups())
+    sent = pl.pallas_call(
+        pack_kernel,
+        out_shape=jax.ShapeDtypeStruct((BLOCKS, width + TERMS, tile), BF),
+        in_specs=[VMEM, VMEM],
+        out_specs=VMEM,
+        compiler_params=params(24),
+        name="pack",
+    )(grads, terms)
+    got = exchange(sent, block_groups())
     sent = pl.pallas_call(
         spread_kernel,
-        out_shape=jax.ShapeDtypeStruct((NEAR, NH * width + 16, tile), BF),
+        out_shape=jax.ShapeDtypeStruct((QUAD, BLOCKS * width + TERMS, tile), BF),
         in_specs=[VMEM],
         out_specs=VMEM,
         compiler_params=params(24),
-        name="spread_near",
+        name="spread_quad",
     )(got)
-    panel = exchange(sent, near_groups())
+    panel = exchange(sent, quad_groups())
     mine, theirs = pl.pallas_call(
         backward_kernel,
-        out_shape=(jax.ShapeDtypeStruct((NZ, width + 16, tile), BF),) * 2,
+        out_shape=(jax.ShapeDtypeStruct((NZ, width + TERMS, tile), BF),) * 2,
         in_specs=[SMEM, SMEM, VMEM, VMEM],
         out_specs=(VMEM, VMEM),
         scratch_shapes=[pltpu.VMEM((col_tiles, width, tile), F32)],
@@ -232,13 +272,15 @@
     got = lax.ppermute(theirs, "core", swap)
     both = (mine.astype(F32) + got.astype(F32)).astype(BF)
     back = exchange(both, depth_groups())
-    back = jnp.sum(back.astype(F32), axis=0)
-    piece = back[width:]
-    grad_features = back[:width].astype(BF).reshape(col_tiles, share, tile)
-    grad_features = grad_features.transpose(0, 2, 1).reshape(nodes, share)
-    whole = jnp.broadcast_to(piece[None], (row_tiles,) + piece.shape)
-    whole = lax.all_to_all(whole, ("y", "x"), 0, 0, tiled=True)
-    grad_weight = whole.reshape(row_tiles, 2, 8, tile).transpose(0, 2, 1, 3).reshape(width, width)
+    grad_features, grad_weight = pl.pallas_call(
+        finish_kernel,
+        out_shape=(jax.ShapeDtypeStruct((share, nodes), BF), jax.ShapeDtypeStruct((width, width), F32)),
+        in_specs=[SMEM, VMEM],
+        out_specs=(VMEM, VMEM),
+        compiler_params=params(24),
+        name="finish",
+    )(info, back)
+    grad_features = grad_features.T
     return (activations, grad_features, grad_weight)
 
 

time: 182 us -> 172 us (0.945)
  waiting for transfers between devices: 27.4 us -> 17.9 us
  starting transfers between devices: 22.6 us -> 14.1 us
  blocking collectives: 117 us -> 123 us
  local copies, waits for them, and re-layouts: 4.67 us -> 1.93 us
  Pallas kernels: 5.92 us -> 8.53 us
    all_to_all x1 -> x0, waiting for transfers between devices: 9.29 us -> none  [body(): whole = lax.all_to_all(whole, ('y', 'x'), 0, 0, tiled=True)]
    all_to_all x1 -> x0, starting transfers between devices: 8.46 us -> none  [body(): whole = lax.all_to_all(whole, ('y', 'x'), 0, 0, tiled=True)]
    all_to_all x5 -> x6, blocking collectives: 117 us -> 123 us  [exchange(): return lax.all_to_all(x, AXES, 0, 0, axis_index_groups=groups, tiled=True)]
    pallas_call x3 -> x5, Pallas kernels: 2.8 us -> 5.08 us  [the longest x1 3.19 us: body(): pl.pallas_call(forward_kernel, out_shape=jax.ShapeDtypeStruct((QUAD, BLOC...]
    all_to_all x1, waiting for transfers between devices: 16.1 us -> 14 us  [exchange(): return lax.all_to_all(x, AXES, 0, 0, axis_index_groups=groups, tiled=True)]
    ppermute x1, waiting for transfers between devices: 0.01 us -> 1.9 us  [body(): other = lax.ppermute(own, 'core', swap)]
  transfers between devices with their start and end apart: 4 -> 3, of which waited for: 3 -> 3; matrix products, arithmetic and copies ran while one was open for 2% -> 2% of each run, Pallas kernels for 0% -> 0%
where the time goes in v2:
time: 172 us; the launch traced here: 169 us
  blocking collectives  123 us (72%)
  waiting for transfers between devices  17.9 us (10%)
  starting transfers between devices  14.1 us (8%)
  Pallas kernels  8.53 us (5%)
  other arithmetic  2.49 us (1%)
  local copies, waits for them, and re-layouts  1.93 us (1%)
    all_to_all x6, blocking collectives, exchange(): return lax.all_to_all(x, AXES, 0, 0, axis_index_groups=groups, tiled=True)  123 us
    all_to_all x1, waiting for transfers between devices, exchange(): return lax.all_to_all(x, AXES, 0, 0, axis_index_groups=groups, tiled=True)  14 us
    all_to_all x1, starting transfers between devices, exchange(): return lax.all_to_all(x, AXES, 0, 0, axis_index_groups=groups, tiled=True)  10.3 us
  transfers between devices with their start and end apart: 3, of which 3 were waited for; matrix products, arithmetic and copies ran while one was open for 2% of the time, Pallas kernels for 0%

profile of v2, /device:TPU:6, one launch (start us, length us, event | category | flops | bytes accessed | tf_op | source)
XLA Modules:
  0.0 169.2 jit_solution(8256412795002922376)
XLA Ops:
  0.6 1.7 broadcast_in_dim.10
  2.3 10.3 %all-to-all-start = ((bf16[8,16,2048]{2,1,0:T(8,128)(2,1)}), bf16[8,16,2048]{2,1,0:T(8,128)(2,1)}, u32[]{:S(2)}, u32[]{:S(2)}) async-start(bf16[8,16,2048]{2,1,0:T(8,128)(2,1)} %broadcast_in_dim.10), calls=%async_computation | async-start | bytes 1048576 | tf_op jit(solution)/shard_map/all_to_all | solution.py:68
  13.3 0.1 pad_add_fusion.1.info
  13.4 2.2 %bitcast_select_fusion.vals = bf16[96,128,128]{2,1,0:T(8,128)(2,1)S(1)} fusion(bf16[1,1,96,128,128]{4,3,2,1,0:T(8,128)(2,1)} %param.9, pred[96]{0:T(512)(128)(4,1)S(1)} %iota_compare_fusion), kind=kLoop, calls=%fused_computation | loop fusion | flops 1572864 | bytes 6291552 | tf_op jit(solution)/shard_map/jit(_where)/select_n | solution.py:210
  15.6 14.0 %all-to-all-done.own = bf16[8,16,2048]{2,1,0:T(8,128)(2,1)} async-done(((bf16[8,16,2048]{2,1,0:T(8,128)(2,1)}), bf16[8,16,2048]{2,1,0:T(8,128)(2,1)}, u32[]{:S(2)}, u32[]{:S(2)}) %all-to-all-start) | async-done | bytes 524320 | tf_op jit(solution)/shard_map/all_to_all | solution.py:68
  29.5 1.9 %collective-permute-start = (bf16[8,16,2048]{2,1,0:T(8,128)(2,1)}, bf16[8,16,2048]{2,1,0:T(8,128)(2,1)}, u32[]{:S(2)}, u32[]{:S(2)}) collective-permute-start(bf16[8,16,2048]{2,1,0:T(8,128)(2,1)} %all-to-all-done.own), channel_id=1, source_target_pairs={{0,32},{32,0},{1,33},{33,1},{2,34},{34,2},{3,35},{35,3},{4,36},{36... | collective-permute-start | bytes 1572872 | tf_op jit(solution)/shard_map/ppermute | solution.py:208
  31.5 0.1 copy.9
  31.6 0.1 reshape.323.coords
  31.8 1.9 %collective-permute-done.other = bf16[8,16,2048]{2,1,0:T(8,128)(2,1)} collective-permute-done((bf16[8,16,2048]{2,1,0:T(8,128)(2,1)}, bf16[8,16,2048]{2,1,0:T(8,128)(2,1)}, u32[]{:S(2)}, u32[]{:S(2)}) %collective-permute-start) | collective-permute-done | bytes 524320 | tf_op jit(solution)/shard_map/ppermute | solution.py:208
  33.7 3.2 %forward_tiles.1 = bf16[4,8,128,256]{3,2,1,0:T(8,128)(2,1)S(1)} custom-call(s32[192]{0:T(256)S(1)} %reshape.323.coords, s32[2]{0:T(128)S(1)} %pad_add_fusion.1.info, bf16[8,16,2048]{2,1,0:T(8,128)(2,1)} %all-to-all-done.own, bf16[8,16,2048]{2,1,0:T(8,128)(2,1)} %collective-permute-done.other, bf16[96,128,128]{2,1,0:T(8,128)(2,1)S(1)} %bitcast_select_fusion.vals), custom_call_target="tpu_custom_call" | custom-call | tf_op jit(solution)/shard_map/forward_tiles/pallas_call | solution.py:212
  36.9 19.2 %all_to_all.35.parts = bf16[4,8,128,256]{3,2,1,0:T(8,128)(2,1)S(1)} all-to-all(bf16[4,8,128,256]{3,2,1,0:T(8,128)(2,1)S(1)} %forward_tiles.1), channel_id=1, replica_groups={{0,1,4,5},{2,3,6,7},{8,9,12,13},{10,11,14,15},{16,17,20,21},{18,19,22,2..., dimensions={0} | all-to-all | bytes 4194304 | tf_op jit(solution)/shard_map/all_to_all | solution.py:68
  56.0 0.3 add_quad.1
  56.3 26.0 %all_to_all.36.parts = bf16[8,128,256]{2,1,0:T(8,128)(2,1)S(1)} all-to-all(bf16[8,128,256]{2,1,0:T(8,128)(2,1)S(1)} %add_quad.1), channel_id=1, replica_groups={{0,2,8,10,16,18,24,26},{1,3,9,11,17,19,25,27},{4,6,12,14,20,22,28,30},{..., dimensions={0} | all-to-all | bytes 1048576 | tf_op jit(solution)/shard_map/all_to_all | solution.py:68
  82.3 1.5 dense.1
  83.8 12.3 %all_to_all.37.terms = bf16[8,64,128]{2,1,0:T(8,128)(2,1)S(1)} all-to-all(bf16[8,64,128]{2,1,0:T(8,128)(2,1)S(1)} %get-tuple-element.18), channel_id=1, replica_groups={{0,64,128,192,256,320,384,448},{1,65,129,193,257,321,385,449},{2,66,130..., dimensions={0} | all-to-all | bytes 262144 | tf_op jit(solution)/shard_map/all_to_all | solution.py:68
  96.2 22.4 %all_to_all.38.got = bf16[8,320,128]{2,1,0:T(8,128)(2,1)S(1)} all-to-all(bf16[8,320,128]{2,1,0:T(8,128)(2,1)S(1)} %pack.1), channel_id=1, replica_groups={{0,2,8,10,16,18,24,26},{1,3,9,11,17,19,25,27},{4,6,12,14,20,22,28,30},{..., dimensions={0} | all-to-all | bytes 1310720 | tf_op jit(solution)/shard_map/all_to_all | solution.py:68
  118.6 0.2 spread_quad.1
  118.8 19.0 %all_to_all.39.panel = bf16[4,2112,128]{2,1,0:T(8,128)(2,1)S(1)} all-to-all(bf16[4,2112,128]{2,1,0:T(8,128)(2,1)S(1)} %spread_quad.1), channel_id=1, replica_groups={{0,1,4,5},{2,3,6,7},{8,9,12,13},{10,11,14,15},{16,17,20,21},{18,19,22,2..., dimensions={0} | all-to-all | bytes 4325376 | tf_op jit(solution)/shard_map/all_to_all | solution.py:68
  137.8 2.0 %backward_tiles.1 = (bf16[8,320,128]{2,1,0:T(8,128)(2,1)S(1)}, bf16[8,320,128]{2,1,0:T(8,128)(2,1)S(1)}) custom-call(s32[192]{0:T(256)S(1)} %reshape.323.coords, s32[2]{0:T(128)S(1)} %pad_add_fusion.1.info, bf16[4,2112,128]{2,1,0:T(8,128)(2,1)S(1)} %all_to_all.39.panel, bf16[96,128,128]{2,1,0:T(8,128)(2,1)S(1)} %bitcast_select_fusion.vals), custom_call_target="tpu_custom_call" | custom-call | tf_op jit(solution)/shard_map/backward_tiles/pallas_call | solution.py:263
  139.9 1.9 %collective-permute-start.1 = (bf16[8,320,128]{2,1,0:T(8,128)(2,1)S(1)}, bf16[8,320,128]{2,1,0:T(8,128)(2,1)S(1)}, u32[]{:S(2)}, u32[]{:S(2)}) collective-permute-start(bf16[8,320,128]{2,1,0:T(8,128)(2,1)S(1)} %get-tuple-element.20), channel_id=1, source_target_pairs={{0,32},{32,0},{1,33},{33,1},{2,34},{34,2},{3,35},{35,3},{4,36},{36... | collective-permute-start | bytes 1966088 | tf_op jit(solution)/shard_map/ppermute | solution.py:272
  141.8 2.1 %collective-permute-done.1 = bf16[8,320,128]{2,1,0:T(8,128)(2,1)S(1)} collective-permute-done((bf16[8,320,128]{2,1,0:T(8,128)(2,1)S(1)}, bf16[8,320,128]{2,1,0:T(8,128)(2,1)S(1)}, u32[]{:S(2)}, u32[]{:S(2)}) %collective-permute-start.1) | collective-permute-done | bytes 655392 | tf_op jit(solution)/shard_map/ppermute | solution.py:272
  143.8 0.2 add_convert_fusion
  144.0 23.8 %all_to_all.40.got = bf16[8,320,128]{2,1,0:T(8,128)(2,1)S(1)} all-to-all(bf16[8,320,128]{2,1,0:T(8,128)(2,1)S(1)} %add_convert_fusion), channel_id=1, replica_groups={{0,64,128,192,256,320,384,448},{1,65,129,193,257,321,385,449},{2,66,130..., dimensions={0} | all-to-all | bytes 1310720 | tf_op jit(solution)/shard_map/all_to_all | solution.py:68
  167.9 1.3 finish.1
  (11 shorter events, 0.1 us)
Async XLA Ops:
  2.3 27.2 %all-to-all-start = ((bf16[8,16,2048]{2,1,0:T(8,128)(2,1)}), bf16[8,16,2048]{2,1,0:T(8,128)(2,1)}, u32[]{:S(2)}, u32[]{:S(2)}) async-start(bf16[8,16,2048]{2,1,0:T(8,128)(2,1)} %broadcast_in_dim.10), calls=%async_computation | async-start | bytes 1048576 | tf_op jit(solution)/shard_map/all_to_all | solution.py:68
  13.4 18.1 %copy-start.2 = (s32[1,1,96,2]{2,3,1,0:T(2,128)S(1)}, s32[1,1,96,2]{2,3,1,0:T(2,128)}, u32[]{:S(2)}) copy-start(s32[1,1,96,2]{2,3,1,0:T(2,128)} %param.10) | copy-start | bytes 2308
  29.5 4.1 %collective-permute-start = (bf16[8,16,2048]{2,1,0:T(8,128)(2,1)}, bf16[8,16,2048]{2,1,0:T(8,128)(2,1)}, u32[]{:S(2)}, u32[]{:S(2)}) collective-permute-start(bf16[8,16,2048]{2,1,0:T(8,128)(2,1)} %all-to-all-done.own), channel_id=1, source_target_pairs={{0,32},{32,0},{1,33},{33,1},{2,34},{34,2},{3,35},{35,3},{4,36},{36... | collective-permute-start | bytes 1572872 | tf_op jit(solution)/shard_map/ppermute | solution.py:208
  56.0 26.3 %copy-start = (bf16[256,256]{1,0:T(8,128)(2,1)S(1)}, bf16[256,256]{1,0:T(8,128)(2,1)}, u32[]{:S(2)}) copy-start(bf16[256,256]{1,0:T(8,128)(2,1)} %weight.1) | copy-start | bytes 393220
  56.0 26.3 %copy-start.1 = (bf16[128,256]{1,0:T(8,128)(2,1)S(1)}, bf16[128,256]{1,0:T(8,128)(2,1)}, u32[]{:S(2)}) copy-start(bf16[128,256]{1,0:T(8,128)(2,1)} %cot.1) | copy-start | bytes 196612
  139.9 4.0 %collective-permute-start.1 = (bf16[8,320,128]{2,1,0:T(8,128)(2,1)S(1)}, bf16[8,320,128]{2,1,0:T(8,128)(2,1)S(1)}, u32[]{:S(2)}, u32[]{:S(2)}) collective-permute-start(bf16[8,320,128]{2,1,0:T(8,128)(2,1)S(1)} %get-tuple-element.20), channel_id=1, source_target_pairs={{0,32},{32,0},{1,33},{33,1},{2,34},{34,2},{3,35},{35,3},{4,36},{36... | collective-permute-start | bytes 1966088 | tf_op jit(solution)/shard_map/ppermute | solution.py:272

commit v3 on v2

--- a/solution.py
+++ b/solution.py
@@ -15,7 +15,7 @@
 QUAD = 4
 BLOCKS = NY * NX // QUAD
 TERMS = 2 * 32
-UNROLL = 8
+UNROLL = 32
 
 
 def device(z, core, y, x):
@@ -203,7 +203,7 @@
 
     own = jnp.broadcast_to(features.T[None], (NZ, share, nodes))
     own = exchange(own, depth_groups())
-    own, count, coords = lax.optimization_barrier((own, tile_count[0, 0], tile_coords))
+    count, coords = tile_count[0, 0], tile_coords
     coords = jnp.stack([spot_of(coords[0, 0, :, 0], core), coords[0, 0, :, 1]], axis=-1).reshape(-1)
     other = lax.ppermute(own, "core", swap)
     live = lax.broadcasted_iota(jnp.int32, (slots, tile, tile), 0) < count

time: 172 us -> 170 us (0.988)
    ppermute x1, waiting for transfers between devices: 1.9 us -> 0.01 us  [body(): other = lax.ppermute(own, 'core', swap)]
  transfers between devices with their start and end apart: 3 -> 3, of which waited for: 3 -> 2; matrix products, arithmetic and copies ran while one was open for 2% -> 2% of each run, Pallas kernels for 0% -> 0%
where the time goes in v3:
time: 170 us; the launch traced here: 168 us
  blocking collectives  122 us (72%)
  waiting for transfers between devices  16.8 us (10%)
  starting transfers between devices  14.1 us (8%)
  Pallas kernels  8.53 us (5%)
  other arithmetic  3.15 us (2%)
  local copies, waits for them, and re-layouts  2.62 us (2%)
    all_to_all x6, blocking collectives, exchange(): return lax.all_to_all(x, AXES, 0, 0, axis_index_groups=groups, tiled=True)  122 us
    all_to_all x1, waiting for transfers between devices, exchange(): return lax.all_to_all(x, AXES, 0, 0, axis_index_groups=groups, tiled=True)  14.7 us
    all_to_all x1, starting transfers between devices, exchange(): return lax.all_to_all(x, AXES, 0, 0, axis_index_groups=groups, tiled=True)  10.3 us
  transfers between devices with their start and end apart: 3, of which 2 were waited for; matrix products, arithmetic and copies ran while one was open for 2% of the time, Pallas kernels for 0%

profile of v3, /device:TPU:6, one launch (start us, length us, event | category | flops | bytes accessed | tf_op | source)
XLA Modules:
  0.0 168.4 jit_solution(8261586229032381782)
XLA Ops:
  0.6 1.7 %broadcast_in_dim.10 = bf16[8,16,2048]{2,1,0:T(8,128)(2,1)} broadcast(bf16[16,2048]{1,0:T(8,128)(2,1)} %bitcast.24), dimensions={1,2} | broadcast | bytes 589824 | tf_op jit(solution)/shard_map/broadcast_in_dim | solution.py:204
  2.3 10.3 %all-to-all-start = ((bf16[8,16,2048]{2,1,0:T(8,128)(2,1)}), bf16[8,16,2048]{2,1,0:T(8,128)(2,1)S(1)}, u32[]{:S(2)}, u32[]{:S(2)}) async-start(bf16[8,16,2048]{2,1,0:T(8,128)(2,1)} %broadcast_in_dim.10), calls=%async_computation | async-start | bytes 1048576 | tf_op jit(solution)/shard_map/all_to_all | solution.py:68
  13.3 0.7 slice_bitcast_fusion
  14.0 0.7 add_add_fusion
  14.7 14.7 %all-to-all-done.own = bf16[8,16,2048]{2,1,0:T(8,128)(2,1)S(1)} async-done(((bf16[8,16,2048]{2,1,0:T(8,128)(2,1)}), bf16[8,16,2048]{2,1,0:T(8,128)(2,1)S(1)}, u32[]{:S(2)}, u32[]{:S(2)}) %all-to-all-start) | async-done | bytes 524320 | tf_op jit(solution)/shard_map/all_to_all | solution.py:68
  29.4 1.9 %collective-permute-start = (bf16[8,16,2048]{2,1,0:T(8,128)(2,1)S(1)}, bf16[8,16,2048]{2,1,0:T(8,128)(2,1)S(1)}, u32[]{:S(2)}, u32[]{:S(2)}) collective-permute-start(bf16[8,16,2048]{2,1,0:T(8,128)(2,1)S(1)} %all-to-all-done.own), channel_id=1, source_target_pairs={{0,32},{32,0},{1,33},{33,1},{2,34},{34,2},{3,35},{35,3},{4,36},{36... | collective-permute-start | bytes 1572872 | tf_op jit(solution)/shard_map/ppermute | solution.py:208
  31.4 0.1 copy.9
  31.5 0.1 reshape.323.coords
  31.7 2.2 %bitcast_select_fusion.vals = bf16[96,128,128]{2,1,0:T(8,128)(2,1)S(1)} fusion(bf16[1,1,96,128,128]{4,3,2,1,0:T(8,128)(2,1)} %param.9, pred[96]{0:T(512)(128)(4,1)S(1)} %iota_compare_fusion), kind=kLoop, calls=%fused_computation | loop fusion | flops 1572864 | bytes 6291552 | tf_op jit(solution)/shard_map/jit(_where)/select_n | solution.py:210
  33.9 2.9 %forward_tiles.1 = bf16[4,8,128,256]{3,2,1,0:T(8,128)(2,1)S(1)} custom-call(s32[192]{0:T(256)S(1)} %reshape.323.coords, s32[2]{0:T(128)S(1)} %pad_add_fusion.1.info, bf16[8,16,2048]{2,1,0:T(8,128)(2,1)S(1)} %all-to-all-done.own, bf16[8,16,2048]{2,1,0:T(8,128)(2,1)S(1)} %collective-permute-done.other, bf16[96,128,128]{2,1,0:T(8,128)(2,1)S(1)} %bitcast_select_fusion.vals), custom_call_target="tpu_custom_call" | custom-call | tf_op jit(solution)/shard_map/forward_tiles/pallas_call | solution.py:212
  36.7 18.6 %all_to_all.35.parts = bf16[4,8,128,256]{3,2,1,0:T(8,128)(2,1)S(1)} all-to-all(bf16[4,8,128,256]{3,2,1,0:T(8,128)(2,1)S(1)} %forward_tiles.1), channel_id=1, replica_groups={{0,1,4,5},{2,3,6,7},{8,9,12,13},{10,11,14,15},{16,17,20,21},{18,19,22,2..., dimensions={0} | all-to-all | bytes 4194304 | tf_op jit(solution)/shard_map/all_to_all | solution.py:68
  55.3 0.3 add_quad.1
  55.6 25.7 %all_to_all.36.parts = bf16[8,128,256]{2,1,0:T(8,128)(2,1)S(1)} all-to-all(bf16[8,128,256]{2,1,0:T(8,128)(2,1)S(1)} %add_quad.1), channel_id=1, replica_groups={{0,2,8,10,16,18,24,26},{1,3,9,11,17,19,25,27},{4,6,12,14,20,22,28,30},{..., dimensions={0} | all-to-all | bytes 1048576 | tf_op jit(solution)/shard_map/all_to_all | solution.py:68
  81.2 1.5 dense.1
  82.7 12.3 %all_to_all.37.terms = bf16[8,64,128]{2,1,0:T(8,128)(2,1)S(1)} all-to-all(bf16[8,64,128]{2,1,0:T(8,128)(2,1)S(1)} %get-tuple-element.12), channel_id=1, replica_groups={{0,64,128,192,256,320,384,448},{1,65,129,193,257,321,385,449},{2,66,130..., dimensions={0} | all-to-all | bytes 262144 | tf_op jit(solution)/shard_map/all_to_all | solution.py:68
  95.1 22.4 %all_to_all.38.got = bf16[8,320,128]{2,1,0:T(8,128)(2,1)S(1)} all-to-all(bf16[8,320,128]{2,1,0:T(8,128)(2,1)S(1)} %pack.1), channel_id=1, replica_groups={{0,2,8,10,16,18,24,26},{1,3,9,11,17,19,25,27},{4,6,12,14,20,22,28,30},{..., dimensions={0} | all-to-all | bytes 1310720 | tf_op jit(solution)/shard_map/all_to_all | solution.py:68
  117.5 0.2 spread_quad.1
  117.7 19.7 %all_to_all.39.panel = bf16[4,2112,128]{2,1,0:T(8,128)(2,1)S(1)} all-to-all(bf16[4,2112,128]{2,1,0:T(8,128)(2,1)S(1)} %spread_quad.1), channel_id=1, replica_groups={{0,1,4,5},{2,3,6,7},{8,9,12,13},{10,11,14,15},{16,17,20,21},{18,19,22,2..., dimensions={0} | all-to-all | bytes 4325376 | tf_op jit(solution)/shard_map/all_to_all | solution.py:68
  137.4 2.3 %backward_tiles.1 = (bf16[8,320,128]{2,1,0:T(8,128)(2,1)S(1)}, bf16[8,320,128]{2,1,0:T(8,128)(2,1)S(1)}) custom-call(s32[192]{0:T(256)S(1)} %reshape.323.coords, s32[2]{0:T(128)S(1)} %pad_add_fusion.1.info, bf16[4,2112,128]{2,1,0:T(8,128)(2,1)S(1)} %all_to_all.39.panel, bf16[96,128,128]{2,1,0:T(8,128)(2,1)S(1)} %bitcast_select_fusion.vals), custom_call_target="tpu_custom_call" | custom-call | tf_op jit(solution)/shard_map/backward_tiles/pallas_call | solution.py:263
  139.7 1.9 %collective-permute-start.1 = (bf16[8,320,128]{2,1,0:T(8,128)(2,1)S(1)}, bf16[8,320,128]{2,1,0:T(8,128)(2,1)S(1)}, u32[]{:S(2)}, u32[]{:S(2)}) collective-permute-start(bf16[8,320,128]{2,1,0:T(8,128)(2,1)S(1)} %get-tuple-element.14), channel_id=1, source_target_pairs={{0,32},{32,0},{1,33},{33,1},{2,34},{34,2},{3,35},{35,3},{4,36},{36... | collective-permute-start | bytes 1966088 | tf_op jit(solution)/shard_map/ppermute | solution.py:272
  141.7 2.1 %collective-permute-done.1 = bf16[8,320,128]{2,1,0:T(8,128)(2,1)S(1)} collective-permute-done((bf16[8,320,128]{2,1,0:T(8,128)(2,1)S(1)}, bf16[8,320,128]{2,1,0:T(8,128)(2,1)S(1)}, u32[]{:S(2)}, u32[]{:S(2)}) %collective-permute-start.1) | collective-permute-done | bytes 655392 | tf_op jit(solution)/shard_map/ppermute | solution.py:272
  143.7 0.2 add_convert_fusion
  143.9 23.1 %all_to_all.40.got = bf16[8,320,128]{2,1,0:T(8,128)(2,1)S(1)} all-to-all(bf16[8,320,128]{2,1,0:T(8,128)(2,1)S(1)} %add_convert_fusion), channel_id=1, replica_groups={{0,64,128,192,256,320,384,448},{1,65,129,193,257,321,385,449},{2,66,130..., dimensions={0} | all-to-all | bytes 1310720 | tf_op jit(solution)/shard_map/all_to_all | solution.py:68
  167.0 1.3 finish.1
  (9 shorter events, 0.2 us)
Async XLA Ops:
  2.3 27.1 %all-to-all-start = ((bf16[8,16,2048]{2,1,0:T(8,128)(2,1)}), bf16[8,16,2048]{2,1,0:T(8,128)(2,1)S(1)}, u32[]{:S(2)}, u32[]{:S(2)}) async-start(bf16[8,16,2048]{2,1,0:T(8,128)(2,1)} %broadcast_in_dim.10), calls=%async_computation | async-start | bytes 1048576 | tf_op jit(solution)/shard_map/all_to_all | solution.py:68
  29.4 4.4 %collective-permute-start = (bf16[8,16,2048]{2,1,0:T(8,128)(2,1)S(1)}, bf16[8,16,2048]{2,1,0:T(8,128)(2,1)S(1)}, u32[]{:S(2)}, u32[]{:S(2)}) collective-permute-start(bf16[8,16,2048]{2,1,0:T(8,128)(2,1)S(1)} %all-to-all-done.own), channel_id=1, source_target_pairs={{0,32},{32,0},{1,33},{33,1},{2,34},{34,2},{3,35},{35,3},{4,36},{36... | collective-permute-start | bytes 1572872 | tf_op jit(solution)/shard_map/ppermute | solution.py:208
  55.3 25.9 %copy-start = (bf16[256,256]{1,0:T(8,128)(2,1)S(1)}, bf16[256,256]{1,0:T(8,128)(2,1)}, u32[]{:S(2)}) copy-start(bf16[256,256]{1,0:T(8,128)(2,1)} %weight.1) | copy-start | bytes 393220
  55.3 25.9 %copy-start.1 = (bf16[128,256]{1,0:T(8,128)(2,1)S(1)}, bf16[128,256]{1,0:T(8,128)(2,1)}, u32[]{:S(2)}) copy-start(bf16[128,256]{1,0:T(8,128)(2,1)} %cot.1) | copy-start | bytes 196612
  139.7 4.0 %collective-permute-start.1 = (bf16[8,320,128]{2,1,0:T(8,128)(2,1)S(1)}, bf16[8,320,128]{2,1,0:T(8,128)(2,1)S(1)}, u32[]{:S(2)}, u32[]{:S(2)}) collective-permute-start(bf16[8,320,128]{2,1,0:T(8,128)(2,1)S(1)} %get-tuple-element.14), channel_id=1, source_target_pairs={{0,32},{32,0},{1,33},{33,1},{2,34},{34,2},{3,35},{35,3},{4,36},{36... | collective-permute-start | bytes 1966088 | tf_op jit(solution)/shard_map/ppermute | solution.py:272

commit v4 on v3

--- a/solution.py
+++ b/solution.py
@@ -15,7 +15,7 @@
 QUAD = 4
 BLOCKS = NY * NX // QUAD
 TERMS = 2 * 32
-UNROLL = 32
+UNROLL = 48
 
 
 def device(z, core, y, x):

time: 170 us -> 170 us (level)
  no operation moved by 1% of the time
where the time goes in v4:
time: 170 us; the launch traced here: 168 us
  blocking collectives  122 us (72%)
  waiting for transfers between devices  16.8 us (10%)
  starting transfers between devices  14.1 us (8%)
  Pallas kernels  7.63 us (4%)
  other arithmetic  3.15 us (2%)
  local copies, waits for them, and re-layouts  2.62 us (2%)
    all_to_all x6, blocking collectives, exchange(): return lax.all_to_all(x, AXES, 0, 0, axis_index_groups=groups, tiled=True)  122 us
    all_to_all x1, waiting for transfers between devices, exchange(): return lax.all_to_all(x, AXES, 0, 0, axis_index_groups=groups, tiled=True)  14.7 us
    all_to_all x1, starting transfers between devices, exchange(): return lax.all_to_all(x, AXES, 0, 0, axis_index_groups=groups, tiled=True)  10.3 us
  transfers between devices with their start and end apart: 3, of which 2 were waited for; matrix products, arithmetic and copies ran while one was open for 2% of the time, Pallas kernels for 0%

profile of v4, /device:TPU:6, one launch (start us, length us, event | category | flops | bytes accessed | tf_op | source)
XLA Modules:
  0.0 168.0 jit_solution(15857729280353593340)
XLA Ops:
  0.6 1.7 %broadcast_in_dim.10 = bf16[8,16,2048]{2,1,0:T(8,128)(2,1)} broadcast(bf16[16,2048]{1,0:T(8,128)(2,1)} %bitcast.24), dimensions={1,2} | broadcast | bytes 589824 | tf_op jit(solution)/shard_map/broadcast_in_dim | solution.py:204
  2.3 10.3 %all-to-all-start = ((bf16[8,16,2048]{2,1,0:T(8,128)(2,1)}), bf16[8,16,2048]{2,1,0:T(8,128)(2,1)S(1)}, u32[]{:S(2)}, u32[]{:S(2)}) async-start(bf16[8,16,2048]{2,1,0:T(8,128)(2,1)} %broadcast_in_dim.10), calls=%async_computation | async-start | bytes 1048576 | tf_op jit(solution)/shard_map/all_to_all | solution.py:68
  13.3 0.7 slice_bitcast_fusion
  14.0 0.7 add_add_fusion
  14.7 14.7 %all-to-all-done.own = bf16[8,16,2048]{2,1,0:T(8,128)(2,1)S(1)} async-done(((bf16[8,16,2048]{2,1,0:T(8,128)(2,1)}), bf16[8,16,2048]{2,1,0:T(8,128)(2,1)S(1)}, u32[]{:S(2)}, u32[]{:S(2)}) %all-to-all-start) | async-done | bytes 524320 | tf_op jit(solution)/shard_map/all_to_all | solution.py:68
  29.4 1.9 %collective-permute-start = (bf16[8,16,2048]{2,1,0:T(8,128)(2,1)S(1)}, bf16[8,16,2048]{2,1,0:T(8,128)(2,1)S(1)}, u32[]{:S(2)}, u32[]{:S(2)}) collective-permute-start(bf16[8,16,2048]{2,1,0:T(8,128)(2,1)S(1)} %all-to-all-done.own), channel_id=1, source_target_pairs={{0,32},{32,0},{1,33},{33,1},{2,34},{34,2},{3,35},{35,3},{4,36},{36... | collective-permute-start | bytes 1572872 | tf_op jit(solution)/shard_map/ppermute | solution.py:208
  31.4 0.1 copy.9
  31.5 0.1 reshape.323.coords
  31.7 2.2 %bitcast_select_fusion.vals = bf16[96,128,128]{2,1,0:T(8,128)(2,1)S(1)} fusion(bf16[1,1,96,128,128]{4,3,2,1,0:T(8,128)(2,1)} %param.9, pred[96]{0:T(512)(128)(4,1)S(1)} %iota_compare_fusion), kind=kLoop, calls=%fused_computation | loop fusion | flops 1572864 | bytes 6291552 | tf_op jit(solution)/shard_map/jit(_where)/select_n | solution.py:210
  33.9 2.4 %forward_tiles.1 = bf16[4,8,128,256]{3,2,1,0:T(8,128)(2,1)S(1)} custom-call(s32[192]{0:T(256)S(1)} %reshape.323.coords, s32[2]{0:T(128)S(1)} %pad_add_fusion.1.info, bf16[8,16,2048]{2,1,0:T(8,128)(2,1)S(1)} %all-to-all-done.own, bf16[8,16,2048]{2,1,0:T(8,128)(2,1)S(1)} %collective-permute-done.other, bf16[96,128,128]{2,1,0:T(8,128)(2,1)S(1)} %bitcast_select_fusion.vals), custom_call_target="tpu_custom_call" | custom-call | tf_op jit(solution)/shard_map/forward_tiles/pallas_call | solution.py:212
  36.3 18.5 %all_to_all.35.parts = bf16[4,8,128,256]{3,2,1,0:T(8,128)(2,1)S(1)} all-to-all(bf16[4,8,128,256]{3,2,1,0:T(8,128)(2,1)S(1)} %forward_tiles.1), channel_id=1, replica_groups={{0,1,4,5},{2,3,6,7},{8,9,12,13},{10,11,14,15},{16,17,20,21},{18,19,22,2..., dimensions={0} | all-to-all | bytes 4194304 | tf_op jit(solution)/shard_map/all_to_all | solution.py:68
  54.8 0.3 add_quad.1
  55.1 25.7 %all_to_all.36.parts = bf16[8,128,256]{2,1,0:T(8,128)(2,1)S(1)} all-to-all(bf16[8,128,256]{2,1,0:T(8,128)(2,1)S(1)} %add_quad.1), channel_id=1, replica_groups={{0,2,8,10,16,18,24,26},{1,3,9,11,17,19,25,27},{4,6,12,14,20,22,28,30},{..., dimensions={0} | all-to-all | bytes 1048576 | tf_op jit(solution)/shard_map/all_to_all | solution.py:68
  80.8 1.5 dense.1
  82.2 12.7 %all_to_all.37.terms = bf16[8,64,128]{2,1,0:T(8,128)(2,1)S(1)} all-to-all(bf16[8,64,128]{2,1,0:T(8,128)(2,1)S(1)} %get-tuple-element.12), channel_id=1, replica_groups={{0,64,128,192,256,320,384,448},{1,65,129,193,257,321,385,449},{2,66,130..., dimensions={0} | all-to-all | bytes 262144 | tf_op jit(solution)/shard_map/all_to_all | solution.py:68
  95.0 22.5 %all_to_all.38.got = bf16[8,320,128]{2,1,0:T(8,128)(2,1)S(1)} all-to-all(bf16[8,320,128]{2,1,0:T(8,128)(2,1)S(1)} %pack.1), channel_id=1, replica_groups={{0,2,8,10,16,18,24,26},{1,3,9,11,17,19,25,27},{4,6,12,14,20,22,28,30},{..., dimensions={0} | all-to-all | bytes 1310720 | tf_op jit(solution)/shard_map/all_to_all | solution.py:68
  117.4 0.2 spread_quad.1
  117.6 19.6 %all_to_all.39.panel = bf16[4,2112,128]{2,1,0:T(8,128)(2,1)S(1)} all-to-all(bf16[4,2112,128]{2,1,0:T(8,128)(2,1)S(1)} %spread_quad.1), channel_id=1, replica_groups={{0,1,4,5},{2,3,6,7},{8,9,12,13},{10,11,14,15},{16,17,20,21},{18,19,22,2..., dimensions={0} | all-to-all | bytes 4325376 | tf_op jit(solution)/shard_map/all_to_all | solution.py:68
  137.3 1.9 %backward_tiles.1 = (bf16[8,320,128]{2,1,0:T(8,128)(2,1)S(1)}, bf16[8,320,128]{2,1,0:T(8,128)(2,1)S(1)}) custom-call(s32[192]{0:T(256)S(1)} %reshape.323.coords, s32[2]{0:T(128)S(1)} %pad_add_fusion.1.info, bf16[4,2112,128]{2,1,0:T(8,128)(2,1)S(1)} %all_to_all.39.panel, bf16[96,128,128]{2,1,0:T(8,128)(2,1)S(1)} %bitcast_select_fusion.vals), custom_call_target="tpu_custom_call" | custom-call | tf_op jit(solution)/shard_map/backward_tiles/pallas_call | solution.py:263
  139.2 1.9 %collective-permute-start.1 = (bf16[8,320,128]{2,1,0:T(8,128)(2,1)S(1)}, bf16[8,320,128]{2,1,0:T(8,128)(2,1)S(1)}, u32[]{:S(2)}, u32[]{:S(2)}) collective-permute-start(bf16[8,320,128]{2,1,0:T(8,128)(2,1)S(1)} %get-tuple-element.14), channel_id=1, source_target_pairs={{0,32},{32,0},{1,33},{33,1},{2,34},{34,2},{3,35},{35,3},{4,36},{36... | collective-permute-start | bytes 1966088 | tf_op jit(solution)/shard_map/ppermute | solution.py:272
  141.1 2.1 %collective-permute-done.1 = bf16[8,320,128]{2,1,0:T(8,128)(2,1)S(1)} collective-permute-done((bf16[8,320,128]{2,1,0:T(8,128)(2,1)S(1)}, bf16[8,320,128]{2,1,0:T(8,128)(2,1)S(1)}, u32[]{:S(2)}, u32[]{:S(2)}) %collective-permute-start.1) | collective-permute-done | bytes 655392 | tf_op jit(solution)/shard_map/ppermute | solution.py:272
  143.2 0.2 add_convert_fusion
  143.3 23.3 %all_to_all.40.got = bf16[8,320,128]{2,1,0:T(8,128)(2,1)S(1)} all-to-all(bf16[8,320,128]{2,1,0:T(8,128)(2,1)S(1)} %add_convert_fusion), channel_id=1, replica_groups={{0,64,128,192,256,320,384,448},{1,65,129,193,257,321,385,449},{2,66,130..., dimensions={0} | all-to-all | bytes 1310720 | tf_op jit(solution)/shard_map/all_to_all | solution.py:68
  166.6 1.3 finish.1
  (9 shorter events, 0.2 us)
Async XLA Ops:
  2.3 27.1 %all-to-all-start = ((bf16[8,16,2048]{2,1,0:T(8,128)(2,1)}), bf16[8,16,2048]{2,1,0:T(8,128)(2,1)S(1)}, u32[]{:S(2)}, u32[]{:S(2)}) async-start(bf16[8,16,2048]{2,1,0:T(8,128)(2,1)} %broadcast_in_dim.10), calls=%async_computation | async-start | bytes 1048576 | tf_op jit(solution)/shard_map/all_to_all | solution.py:68
  29.4 4.4 %collective-permute-start = (bf16[8,16,2048]{2,1,0:T(8,128)(2,1)S(1)}, bf16[8,16,2048]{2,1,0:T(8,128)(2,1)S(1)}, u32[]{:S(2)}, u32[]{:S(2)}) collective-permute-start(bf16[8,16,2048]{2,1,0:T(8,128)(2,1)S(1)} %all-to-all-done.own), channel_id=1, source_target_pairs={{0,32},{32,0},{1,33},{33,1},{2,34},{34,2},{3,35},{35,3},{4,36},{36... | collective-permute-start | bytes 1572872 | tf_op jit(solution)/shard_map/ppermute | solution.py:208
  54.8 25.9 %copy-start = (bf16[256,256]{1,0:T(8,128)(2,1)S(1)}, bf16[256,256]{1,0:T(8,128)(2,1)}, u32[]{:S(2)}) copy-start(bf16[256,256]{1,0:T(8,128)(2,1)} %weight.1) | copy-start | bytes 393220
  54.8 25.9 %copy-start.1 = (bf16[128,256]{1,0:T(8,128)(2,1)S(1)}, bf16[128,256]{1,0:T(8,128)(2,1)}, u32[]{:S(2)}) copy-start(bf16[128,256]{1,0:T(8,128)(2,1)} %cot.1) | copy-start | bytes 196612
  139.2 4.0 %collective-permute-start.1 = (bf16[8,320,128]{2,1,0:T(8,128)(2,1)S(1)}, bf16[8,320,128]{2,1,0:T(8,128)(2,1)S(1)}, u32[]{:S(2)}, u32[]{:S(2)}) collective-permute-start(bf16[8,320,128]{2,1,0:T(8,128)(2,1)S(1)} %get-tuple-element.14), channel_id=1, source_target_pairs={{0,32},{32,0},{1,33},{33,1},{2,34},{34,2},{3,35},{35,3},{4,36},{36... | collective-permute-start | bytes 1966088 | tf_op jit(solution)/shard_map/ppermute | solution.py:272
